TPU v7x, 32 devices: a whole 2x2x4 slice. The times are simulated.
32 devices in a mesh: gx: 4 (over y, core), gy: 8 (over z, x).
Axes of the slice: x: 2, y: 2, z: 4, core: 2. Of those that a mesh axis runs over, the one named last changes fastest.
Arguments:
- adjoint_in: float32 [19, 4, 64, 1024], P(None, None, 'gx', 'gy'), may hold values from -6 to 6
- forward_pops: bfloat16 [2, 19, 4, 64, 1024], P(None, None, None, 'gx', 'gy'), may hold values from 0 to 0.42, as said below
- solid_mask: int32 [4, 64, 1024], P(None, 'gx', 'gy'), may hold values 0 or 1
- region_label: int32 [64, 1024], P('gx', 'gy'), may hold values from 0 to 2
- design: float32 [64, 1024], P('gx', 'gy'), may hold values from 0 to 1
Outputs:
- adjoint_out: float32 [19, 4, 64, 1024], P(None, None, 'gx', 'gy')
- sensitivity: float32 [64, 1024], P('gx', 'gy')
Inputs may be any that keep to these rules, and one draw needn't show every extreme that they name: `forward_pops`: each population lies between 0.75 and 1.25 times its lattice weight.
All inputs are finite; a program needn't handle non-finite values. No bound on the sum of `solid_mask` on one device may be relied on, other than what follows from the above.
Results may differ from a plain program's by a relative error of at most 0.0004.
Values sent between devices are 32-bit elements; how exact they have to be, the bound alone decides.
A program may use at most 128 MiB of HBM per device.

v0:
```python
import jax
import jax.numpy as jnp
from jax import lax
from jax.sharding import PartitionSpec as P

SWEEPS = 4


VELOCITIES = [
    (0, 0, 0),
    (1, 0, 0),
    (-1, 0, 0),
    (0, 1, 0),
    (0, -1, 0),
    (0, 0, 1),
    (0, 0, -1),
    (1, 1, 0),
    (-1, -1, 0),
    (1, -1, 0),
    (-1, 1, 0),
    (1, 0, 1),
    (-1, 0, -1),
    (1, 0, -1),
    (-1, 0, 1),
    (0, 1, 1),
    (0, -1, -1),
    (0, 1, -1),
    (0, -1, 1),
]
OPPOSITE = [0, 2, 1, 4, 3, 6, 5, 8, 7, 10, 9, 12, 11, 14, 13, 16, 15, 18, 17]
WEIGHTS = [1.0 / 3.0] + [1.0 / 18.0] * 6 + [1.0 / 36.0] * 12
RELAX_RATES = [0.0] * 4 + [1.6] * 6 + [1.4] * 6 + [1.2] * 3
EXPONENTS = [
    (0, 0, 0),
    (1, 0, 0),
    (0, 1, 0),
    (0, 0, 1),
    (2, 0, 0),
    (0, 2, 0),
    (0, 0, 2),
    (1, 1, 0),
    (1, 0, 1),
    (0, 1, 1),
    (2, 1, 0),
    (2, 0, 1),
    (1, 2, 0),
    (0, 2, 1),
    (1, 0, 2),
    (0, 1, 2),
    (2, 2, 0),
    (2, 0, 2),
    (0, 2, 2),
]
BLOCK_LIMIT = 0.5
SENSE_SCALE = 20.0
FILTER_WEIGHT = 16.0


def extended(cells, sides, width):
    for axis, dim in sides:
        count = lax.axis_size(axis)
        ends = count - 1
        head = lax.slice_in_dim(cells, 0, width, axis=dim)
        tail = lax.slice_in_dim(cells, cells.shape[dim] - width, cells.shape[dim], axis=dim)
        cells = jnp.concatenate(
            [
                lax.ppermute(tail, axis, [(i, (i + 1) % count) for i in range(ends)]),
                cells,
                lax.ppermute(head, axis, [((i + 1) % count, i) for i in range(ends)]),
            ],
            axis=dim,
        )
    return cells


def moment_table():
    rows_out = []
    for expo in EXPONENTS:
        vector = [
            float(vel[0] ** expo[0] * vel[1] ** expo[1] * vel[2] ** expo[2]) for vel in VELOCITIES
        ]
        for prior in rows_out:
            factor = sum((a * b for a, b in zip(vector, prior))) / sum((b * b for b in prior))
            vector = [a - factor * b for a, b in zip(vector, prior)]
        rows_out.append(vector)
    norms = [sum((b * b for b in row)) for row in rows_out]
    table = []
    for first in range(19):
        line = []
        for second in range(19):
            line.append(
                sum(
                    (
                        rows_out[k][first] / norms[k] * RELAX_RATES[k] * rows_out[k][second]
                        for k in range(19)
                    )
                )
            )
        table.append(line)
    return table


def collide(popul, blocking):
    relax_matrix = jnp.asarray(moment_table(), jnp.float32)
    veloc = jnp.asarray(VELOCITIES, jnp.float32)
    weights = jnp.asarray(WEIGHTS, jnp.float32)
    density = jnp.sum(popul, axis=0)
    momentum = jnp.dot(veloc.T, popul, precision=lax.Precision.HIGHEST)
    velocity = momentum / density
    along_u = jnp.dot(veloc, velocity, precision=lax.Precision.HIGHEST)
    speed_sq = jnp.sum(velocity * velocity, axis=0)
    equilib = (
        weights[:, None]
        * density
        * (1.0 + 3.0 * along_u + 4.5 * along_u * along_u - 1.5 * speed_sq)
    )
    relaxed = popul - jnp.dot(relax_matrix, popul - equilib, precision=lax.Precision.HIGHEST)
    reflected = popul[jnp.asarray(OPPOSITE, jnp.int32)]
    return ((1.0 - blocking) * relaxed + blocking * reflected, reflected - relaxed)


def adjoint_cell(saved_now, pulled, blocking, lever):

    def forward(popul):
        return collide(popul, blocking)

    _, back_fn, change = jax.vjp(forward, saved_now, has_aux=True)
    (result,) = back_fn(pulled)
    term = jnp.sum(pulled * change, axis=0) * lever
    return (result, term)


def pull_back(padded, width_x, width_y):
    pieces = []
    for slot in range(19):
        step_x, step_y, step_z = VELOCITIES[slot]
        piece = padded[
            slot, :, 1 + step_x : 1 + step_x + width_x, 1 + step_y : 1 + step_y + width_y
        ]
        pieces.append(jnp.roll(piece, -step_z, axis=0))
    return jnp.stack(pieces)


def framed_adjoint(adjoint):
    return extended(adjoint, (("gx", 2), ("gy", 3)), 1)


def helmholtz(raw):
    scale_den = 1.0 + 4.0 * FILTER_WEIGHT
    smooth = raw
    for sweep in range(SWEEPS):
        framed = extended(smooth, (("gx", 0), ("gy", 1)), 1)
        beside_all = framed[:-2, 1:-1] + framed[2:, 1:-1] + framed[1:-1, :-2] + framed[1:-1, 2:]
        smooth = (raw + FILTER_WEIGHT * beside_all) / scale_den
    return smooth


def per_device(adjoint_in, forward_pops, solid_mask, region_label, design):
    planes, width_x, width_y = solid_mask.shape
    inside = region_label > 0
    blocking = jnp.where(
        solid_mask == 1, 1.0, jnp.where(inside[None], BLOCK_LIMIT * design[None], 0.0)
    )
    lever = jnp.where((solid_mask == 0) & inside[None], BLOCK_LIMIT, 0.0).astype(jnp.float32)
    adjoint = adjoint_in
    raw = jnp.zeros((width_x, width_y), jnp.float32)
    for section in (1, 0):
        pulled = pull_back(framed_adjoint(adjoint), width_x, width_y)
        saved_now = forward_pops[section].astype(jnp.float32)
        result, term = adjoint_cell(
            saved_now.reshape(19, -1),
            pulled.reshape(19, -1),
            blocking.reshape(-1),
            lever.reshape(-1),
        )
        adjoint = result.reshape(19, planes, width_x, width_y)
        raw = raw + jnp.sum(term.reshape(planes, width_x, width_y), axis=0)
    raw = SENSE_SCALE * raw
    smooth = helmholtz(raw)
    region_one = (region_label == 1).astype(jnp.float32)
    region_two = (region_label == 2).astype(jnp.float32)
    region_sums, region_counts = lax.psum(
        (
            jnp.stack([jnp.sum(smooth * region_one), jnp.sum(smooth * region_two)]),
            jnp.stack([jnp.sum(region_one), jnp.sum(region_two)]),
        ),
        ("gx", "gy"),
    )
    means = region_sums / jnp.maximum(region_counts, 1.0)
    sensitivity = region_one * (smooth - means[0]) + region_two * (smooth - means[1])
    return (adjoint, sensitivity)


def solution(mesh):
    in_specs = (
        P(None, None, "gx", "gy"),
        P(None, None, None, "gx", "gy"),
        P(None, "gx", "gy"),
        P("gx", "gy"),
        P("gx", "gy"),
    )
    out_specs = (P(None, None, "gx", "gy"), P("gx", "gy"))
    return jax.shard_map(
        per_device, mesh=mesh, in_specs=in_specs, out_specs=out_specs, check_vma=False
    )
```

profile of v0, /device:TPU:0, one launch (start us, length us, event | category | flops | bytes accessed | tf_op | source)
XLA Modules:
  0.0 238.3 jit_solution(5144111084341191548)
XLA Ops:
  2.5 3.0 %collective-permute-start.1 = (f32[19,4,1,128]{3,0,2,1:T(8,128)}, f32[19,4,1,128]{3,0,2,1:T(8,128)}, u32[]{:S(2)}, u32[]{:S(2)}) collective-permute-start(f32[19,4,1,128]{3,0,2,1:T(8,128)} %copy.101), channel_id=1, source_target_pairs={{0,8},{8,16},{16,24},{1,9},{9,17},{17,25},{2,10},{10,18},{18,26},{... | collective-permute-start | bytes 116744 | tf_op jit(solution)/shard_map/ppermute | solution.py:67
  7.4 2.0 constant_dynamic-update-slice_fusion
  13.6 2.4 %fusion.112 = f32[19,8192]{1,0:T(8,128)} fusion(f32[19,3]{1,0:T(8,128)} %constant.52.clone, f32[3,8192]{1,0:T(4,128)S(1)} %get-tuple-element.114, f32[8192]{0:T(1024)S(1)} %bitcast.164), kind=kOutput, calls=%fused_computation.275 | convolution fusion | flops 5627904 | bytes 753892 | tf_op jit(solution)/shard_map/jvp()/dot_general | solution.py:110
  17.3 1.7 fusion.113
  20.2 4.1 %copy.90 = f32[19,4,16,128]{2,0,3,1:T(8,128)} copy(f32[19,4,16,128]{3,2,1,0:T(8,128)S(1)} %copy-done.1) | data formatting | bytes 1245184 | tf_op args[0]
  24.5 1.6 gather_fusion.1
  26.1 1.6 gather_fusion
  29.4 2.6 %dynamic-update-slice.3 = f32[19,4,17,128]{3,2,1,0:T(8,128)} dynamic-update-slice(f32[19,4,17,128]{3,2,1,0:T(8,128)} %constant_dynamic-update-slice_fusion, f32[19,4,1,128]{3,2,1,0:T(1,128)S(1)} %copy.86, s32[]{} %constant.99, s32[]{} %constant.99, s32[]{} %constant.100, s32[]{} %constant.99) | dynamic-update-slice | bytes 77828 | tf_op jit(solution)/shard_map/concatenate | solution.py:65
  34.2 5.0 %copy.89 = f32[19,4,1,128]{2,0,3,1:T(8,128)} copy(f32[19,4,1,128]{3,0,2,1:T(8,128)} %collective-permute-done.1) | data formatting | bytes 77824 | tf_op jit(solution)/shard_map/ppermute | solution.py:67
  39.2 4.9 %copy.91 = f32[19,4,1,128]{2,0,3,1:T(8,128)} copy(f32[19,4,1,128]{3,0,2,1:T(8,128)} %collective-permute-done) | data formatting | bytes 77824 | tf_op jit(solution)/shard_map/ppermute | solution.py:69
  44.1 8.1 %pad_maximum_fusion = f32[19,4,18,128]{2,0,3,1:T(8,128)S(1)} fusion(f32[19,4,1,128]{2,0,3,1:T(8,128)} %copy.91, f32[19,4,16,128]{2,0,3,1:T(8,128)} %copy.90, f32[19,4,1,128]{2,0,3,1:T(8,128)} %copy.89), kind=kLoop, calls=%fused_computation.16 | loop fusion | flops 350208 | bytes 1400832 | tf_op jit(solution)/shard_map/concatenate | solution.py:65
  52.3 2.7 %copy-done = f32[19,4,18,128]{2,0,3,1:T(8,128)} copy-done((f32[19,4,18,128]{2,0,3,1:T(8,128)}, f32[19,4,18,128]{2,0,3,1:T(8,128)S(1)}, u32[]{:S(2)}) %copy-start) | copy-done | bytes 700440
  56.2 5.5 %collective-permute-start.3 = (f32[19,4,18,1]{2,0,3,1:T(8,128)S(1)}, f32[19,4,18,1]{2,0,3,1:T(8,128)}, u32[]{:S(2)}, u32[]{:S(2)}) collective-permute-start(f32[19,4,18,1]{2,0,3,1:T(8,128)S(1)} %get-tuple-element.21), channel_id=1, source_target_pairs={{0,1},{1,2},{2,3},{3,4},{4,5},{5,6},{6,7},{8,9},{9,10},{10,11},{11... | collective-permute-start | bytes 16424 | tf_op jit(solution)/shard_map/ppermute | solution.py:67
  63.6 4.5 %copy.92 = f32[19,4,18,128]{3,0,2,1:T(8,128)S(1)} copy(f32[19,4,18,128]{2,0,3,1:T(8,128)} %copy-done) | data formatting | bytes 1400832 | tf_op jit(solution)/shard_map/concatenate | solution.py:65
  68.1 1.4 slice.687
  70.2 1.5 copy.94
  73.6 2.6 %stack.155 = f32[19,8192]{1,0:T(8,128)S(1)} concatenate(f32[1,8192]{1,0:T(1,128)} %bitcast.186, f32[1,8192]{1,0:T(1,128)} %bitcast.193, f32[1,8192]{1,0:T(1,128)} %bitcast.185, f32[1,8192]{1,0:T(1,128)} %bitcast.176, f32[1,8192]{1,0:T(1,128)} %bitcast.177, f32[1,8192]{1,0:T(1,128)} %bitcast.203, f32[1,8192]{1,0:T(1,128)} %bitcast.204, f32[1,8192]{1,0:T(1,128)} %bitcast.175, ...), dimensions={0} | concatenate | bytes 1245184 | tf_op jit(solution)/shard_map/stack | solution.py:141
  76.2 2.4 %fusion.38 = (f32[8192]{0:T(1024)S(1)}, f32[8192]{0:T(1024)S(1)}, f32[19,8192]{1,0:T(8,128)S(1)}) fusion(f32[8192]{0:T(1024)S(1)} %bitcast.165, f32[19]{0:T(128)} %constant.53.clone, f32[8192]{0:T(1024)} %get-tuple-element.129, f32[19,8192]{1,0:T(8,128)} %fusion.112, f32[19,19]{1,0:T(8,128)} %constant.16.clone, f32[19,8192]{1,0:T(8,128)S(1)} %stack.155, ...), kind=kOutput, calls=%fused_computation.56 | convolution fusion | flops 37806080 | bytes 2033136 | tf_op jit(solution)/shard_map/transpose(jvp())/dot_general | solution.py:117
  78.7 2.1 multiply_reduce_fusion.4
  80.8 1.6 fusion.3
  82.4 1.8 scatter_custom_fusion
  87.4 4.3 %collective-permute-start.5 = (f32[19,4,1,128]{3,2,1,0:T(1,128)S(1)}, f32[19,4,1,128]{3,2,1,0:T(1,128)S(1)}, u32[]{:S(2)}, u32[]{:S(2)}) collective-permute-start(f32[19,4,1,128]{3,2,1,0:T(1,128)S(1)} %get-tuple-element.85), channel_id=1, source_target_pairs={{0,8},{8,16},{16,24},{1,9},{9,17},{17,25},{2,10},{10,18},{18,26},{... | collective-permute-start | bytes 116744 | tf_op jit(solution)/shard_map/ppermute | solution.py:67
  91.8 2.5 %fusion.7 = f32[8192]{0:T(1024)S(1)} fusion(f32[19,8192]{1,0:T(8,128)S(1)} %stack.155, f32[19,8192]{1,0:T(8,128)} %gather_fusion, f32[19,19]{1,0:T(8,128)S(1)} %copy-done.12, f32[19,8192]{1,0:T(8,128)} %fusion.112, f32[8192]{0:T(1024)S(1)} %copy-done.6, f32[8192]{0:T(1024)S(1)} %bitcast.168, f32[19]{0:T(128)S(1)} %copy-done.16, ...), kind=kOutput, calls=%fused_computation.18 | convolution fusion | flops 37814272 | bytes 2278896 | tf_op jit(solution)/shard_map/jvp()/dot_general | solution.py:117
  94.3 2.6 %dynamic-update-slice.1 = f32[19,4,17,128]{3,2,1,0:T(8,128)} dynamic-update-slice(f32[19,4,17,128]{3,2,1,0:T(8,128)} %constant_dynamic-update-slice_fusion.1, f32[19,4,1,128]{3,2,1,0:T(1,128)S(1)} %collective-permute-done.4, s32[]{} %constant.99, s32[]{} %constant.99, s32[]{} %constant.100, s32[]{} %constant.99) | dynamic-update-slice | bytes 77828 | tf_op jit(solution)/shard_map/concatenate | solution.py:65
  101.4 5.2 %collective-permute-start.7 = (f32[19,4,18,1]{0,1,3,2:T(4,128)S(1)}, f32[19,4,18,1]{0,1,3,2:T(4,128)}, u32[]{:S(2)}, u32[]{:S(2)}) collective-permute-start(f32[19,4,18,1]{0,1,3,2:T(4,128)S(1)} %copy.98), channel_id=1, source_target_pairs={{0,1},{1,2},{2,3},{3,4},{4,5},{5,6},{6,7},{8,9},{9,10},{10,11},{11... | collective-permute-start | bytes 16424 | tf_op jit(solution)/shard_map/ppermute | solution.py:67
  108.5 1.8 copy.99
  112.7 2.5 %stack.174 = f32[19,8192]{1,0:T(8,128)S(1)} concatenate(f32[1,8192]{1,0:T(1,128)S(1)} %copy-done.9, f32[1,8192]{1,0:T(1,128)S(1)} %bitcast.192, f32[1,8192]{1,0:T(1,128)S(1)} %bitcast.183, f32[1,8192]{1,0:T(1,128)S(1)} %bitcast.182, f32[1,8192]{1,0:T(1,128)} %bitcast.211, f32[1,8192]{1,0:T(1,128)S(1)} %bitcast.188, f32[1,8192]{1,0:T(1,128)S(1)} %bitcast.187, ...), dimensions={0} | concatenate | bytes 1245184 | tf_op jit(solution)/shard_map/stack | solution.py:141
  115.3 2.3 fusion.39
  117.7 2.3 fusion.6
  120.0 3.9 %collective-permute-start.8 = (f32[1,128]{1,0:T(1,128)S(1)}, f32[1,128]{1,0:T(1,128)S(1)}, u32[]{:S(2)}, u32[]{:S(2)}) collective-permute-start(f32[1,128]{1,0:T(1,128)S(1)} %get-tuple-element.109), channel_id=1, source_target_pairs={{0,8},{8,16},{16,24},{1,9},{9,17},{17,25},{2,10},{10,18},{18,26},{... | collective-permute-start | bytes 1544 | tf_op jit(solution)/shard_map/ppermute | solution.py:67
  125.2 2.0 collective-permute-done.9
  127.3 4.4 %collective-permute-start.10 = (f32[18,1]{1,0:T(8,128)S(1)}, f32[18,1]{1,0:T(8,128)S(1)}, u32[]{:S(2)}, u32[]{:S(2)}) collective-permute-start(f32[18,1]{1,0:T(8,128)S(1)} %get-tuple-element.101), channel_id=1, source_target_pairs={{0,1},{1,2},{2,3},{3,4},{4,5},{5,6},{6,7},{8,9},{9,10},{10,11},{11... | collective-permute-start | bytes 224 | tf_op jit(solution)/shard_map/ppermute | solution.py:67
  133.1 4.9 %collective-permute-done.11 = f32[18,1]{1,0:T(8,128)S(1)} collective-permute-done((f32[18,1]{1,0:T(8,128)S(1)}, f32[18,1]{1,0:T(8,128)S(1)}, u32[]{:S(2)}, u32[]{:S(2)}) %collective-permute-start.11) | collective-permute-done | bytes 104 | tf_op jit(solution)/shard_map/ppermute | solution.py:69
  138.1 3.1 %collective-permute-start.12 = (f32[1,128]{1,0:T(1,128)S(1)}, f32[1,128]{1,0:T(1,128)S(1)}, u32[]{:S(2)}, u32[]{:S(2)}) collective-permute-start(f32[1,128]{1,0:T(1,128)S(1)} %get-tuple-element.107), channel_id=1, source_target_pairs={{0,8},{8,16},{16,24},{1,9},{9,17},{17,25},{2,10},{10,18},{18,26},{... | collective-permute-start | bytes 1544 | tf_op jit(solution)/shard_map/ppermute | solution.py:67
  142.5 2.1 multiply_reduce_fusion.2
  145.1 4.8 %collective-permute-start.14 = (f32[18,1]{1,0:T(8,128)S(1)}, f32[18,1]{1,0:T(8,128)S(1)}, u32[]{:S(2)}, u32[]{:S(2)}) collective-permute-start(f32[18,1]{1,0:T(8,128)S(1)} %get-tuple-element.99), channel_id=1, source_target_pairs={{0,1},{1,2},{2,3},{3,4},{4,5},{5,6},{6,7},{8,9},{9,10},{10,11},{11... | collective-permute-start | bytes 224 | tf_op jit(solution)/shard_map/ppermute | solution.py:67
  151.3 4.2 %collective-permute-done.15 = f32[18,1]{1,0:T(8,128)S(1)} collective-permute-done((f32[18,1]{1,0:T(8,128)S(1)}, f32[18,1]{1,0:T(8,128)S(1)}, u32[]{:S(2)}, u32[]{:S(2)}) %collective-permute-start.15) | collective-permute-done | bytes 104 | tf_op jit(solution)/shard_map/ppermute | solution.py:69
  155.6 2.8 %collective-permute-start.16 = (f32[1,128]{1,0:T(1,128)S(1)}, f32[1,128]{1,0:T(1,128)S(1)}, u32[]{:S(2)}, u32[]{:S(2)}) collective-permute-start(f32[1,128]{1,0:T(1,128)S(1)} %get-tuple-element.105), channel_id=1, source_target_pairs={{0,8},{8,16},{16,24},{1,9},{9,17},{17,25},{2,10},{10,18},{18,26},{... | collective-permute-start | bytes 1544 | tf_op jit(solution)/shard_map/ppermute | solution.py:67
  159.7 3.5 %collective-permute-done.17 = f32[1,128]{1,0:T(1,128)S(1)} collective-permute-done((f32[1,128]{1,0:T(1,128)S(1)}, f32[1,128]{1,0:T(1,128)S(1)}, u32[]{:S(2)}, u32[]{:S(2)}) %collective-permute-start.17) | collective-permute-done | bytes 544 | tf_op jit(solution)/shard_map/ppermute | solution.py:69
  163.3 2.9 %collective-permute-start.18 = (f32[18,1]{1,0:T(8,128)S(1)}, f32[18,1]{1,0:T(8,128)S(1)}, u32[]{:S(2)}, u32[]{:S(2)}) collective-permute-start(f32[18,1]{1,0:T(8,128)S(1)} %get-tuple-element.97), channel_id=1, source_target_pairs={{0,1},{1,2},{2,3},{3,4},{4,5},{5,6},{6,7},{8,9},{9,10},{10,11},{11... | collective-permute-start | bytes 224 | tf_op jit(solution)/shard_map/ppermute | solution.py:67
  167.7 4.2 %collective-permute-done.19 = f32[18,1]{1,0:T(8,128)S(1)} collective-permute-done((f32[18,1]{1,0:T(8,128)S(1)}, f32[18,1]{1,0:T(8,128)S(1)}, u32[]{:S(2)}, u32[]{:S(2)}) %collective-permute-start.19) | collective-permute-done | bytes 104 | tf_op jit(solution)/shard_map/ppermute | solution.py:69
  171.9 3.1 %collective-permute-start.20 = (f32[1,128]{1,0:T(1,128)S(1)}, f32[1,128]{1,0:T(1,128)S(1)}, u32[]{:S(2)}, u32[]{:S(2)}) collective-permute-start(f32[1,128]{1,0:T(1,128)S(1)} %get-tuple-element.103), channel_id=1, source_target_pairs={{0,8},{8,16},{16,24},{1,9},{9,17},{17,25},{2,10},{10,18},{18,26},{... | collective-permute-start | bytes 1544 | tf_op jit(solution)/shard_map/ppermute | solution.py:67
  177.2 1.8 scatter_custom_fusion.1
  179.2 4.5 %collective-permute-start.22 = (f32[18,1]{1,0:T(8,128)S(1)}, f32[18,1]{1,0:T(8,128)S(1)}, u32[]{:S(2)}, u32[]{:S(2)}) collective-permute-start(f32[18,1]{1,0:T(8,128)S(1)} %get-tuple-element.95), channel_id=1, source_target_pairs={{0,1},{1,2},{2,3},{3,4},{4,5},{5,6},{6,7},{8,9},{9,10},{10,11},{11... | collective-permute-start | bytes 224 | tf_op jit(solution)/shard_map/ppermute | solution.py:67
  185.2 4.2 %collective-permute-done.23 = f32[18,1]{1,0:T(8,128)S(1)} collective-permute-done((f32[18,1]{1,0:T(8,128)S(1)}, f32[18,1]{1,0:T(8,128)S(1)}, u32[]{:S(2)}, u32[]{:S(2)}) %collective-permute-start.23) | collective-permute-done | bytes 104 | tf_op jit(solution)/shard_map/ppermute | solution.py:69
  190.2 1.4 pad_maximum_fusion.89
  193.8 42.0 %all-reduce = (f32[2]{0:T(128)S(1)}, f32[2]{0:T(128)S(1)}) all-reduce(f32[2]{0:T(128)S(1)} %pad_maximum_fusion.88, f32[2]{0:T(128)S(1)} %pad_maximum_fusion.89), channel_id=1, replica_groups=mesh['gx'=4,'gy'=8] {'gx','gy'}, use_global_device_ids=true, to_apply=%region_18.19 | all-reduce | flops 4 | bytes 32 | tf_op jit(solution)/shard_map/psum | solution.py:182
  236.4 1.9 select_add_fusion
  (161 shorter events, 48.4 us)
Async XLA Ops:
  0.6 16.2 %copy-start.4 = (f32[19,3]{1,0:T(8,128)S(1)}, f32[19,3]{1,0:T(8,128)}, u32[]{:S(2)}) copy-start(f32[19,3]{1,0:T(8,128)} %constant.52.clone) | copy-start | bytes 688
  0.6 19.6 %copy-start.17 = (s32[19]{0:T(128)S(1)}, s32[19]{0:T(128)}, u32[]{:S(2)}) copy-start(s32[19]{0:T(128)} %constant.59) | copy-start | bytes 232
  0.7 19.6 %copy-start.1 = (f32[19,4,16,128]{3,2,1,0:T(8,128)S(1)}, f32[19,4,16,128]{3,2,1,0:T(8,128)}, u32[]{:S(2)}) copy-start(f32[19,4,16,128]{3,2,1,0:T(8,128)} %param.13) | copy-start | bytes 1867780
  0.7 18.9 %copy-start.13 = (s32[16,128]{1,0:T(8,128)S(1)}, s32[16,128]{1,0:T(8,128)}, u32[]{:S(2)}) copy-start(s32[16,128]{1,0:T(8,128)} %param.16) | copy-start | bytes 24580
  0.7 18.9 %copy-start.15 = (f32[16,128]{1,0:T(8,128)S(1)}, f32[16,128]{1,0:T(8,128)}, u32[]{:S(2)}) copy-start(f32[16,128]{1,0:T(8,128)} %param.17) | copy-start | bytes 24580
  0.7 18.9 %copy-start.7 = (s32[4,16,128]{2,1,0:T(8,128)S(1)}, s32[4,16,128]{2,1,0:T(8,128)}, u32[]{:S(2)}) copy-start(s32[4,16,128]{2,1,0:T(8,128)} %param.15) | copy-start | bytes 98308
  2.5 25.2 %collective-permute-start.1 = (f32[19,4,1,128]{3,0,2,1:T(8,128)}, f32[19,4,1,128]{3,0,2,1:T(8,128)}, u32[]{:S(2)}, u32[]{:S(2)}) collective-permute-start(f32[19,4,1,128]{3,0,2,1:T(8,128)} %copy.101), channel_id=1, source_target_pairs={{0,8},{8,16},{16,24},{1,9},{9,17},{17,25},{2,10},{10,18},{18,26},{... | collective-permute-start | bytes 116744 | tf_op jit(solution)/shard_map/ppermute | solution.py:67
  6.1 22.5 %collective-permute-start = (f32[19,4,1,128]{3,0,2,1:T(8,128)}, f32[19,4,1,128]{3,0,2,1:T(8,128)}, u32[]{:S(2)}, u32[]{:S(2)}) collective-permute-start(f32[19,4,1,128]{3,0,2,1:T(8,128)} %copy.100), channel_id=1, source_target_pairs={{8,0},{16,8},{24,16},{9,1},{17,9},{25,17},{10,2},{18,10},{26,18},{... | collective-permute-start | bytes 116744 | tf_op jit(solution)/shard_map/ppermute | solution.py:69
  13.6 10.9 %copy-start.11 = (f32[3,8192]{1,0:T(4,128)}, f32[3,8192]{1,0:T(4,128)S(1)}, u32[]{:S(2)}) copy-start(f32[3,8192]{1,0:T(4,128)S(1)} %get-tuple-element.114) | copy-start | bytes 294916
  17.2 8.8 %copy-start.10 = (f32[3,8192]{1,0:T(4,128)}, f32[3,8192]{1,0:T(4,128)S(1)}, u32[]{:S(2)}) copy-start(f32[3,8192]{1,0:T(4,128)S(1)} %get-tuple-element.119) | copy-start | bytes 294916
  52.3 2.7 %copy-start = (f32[19,4,18,128]{2,0,3,1:T(8,128)}, f32[19,4,18,128]{2,0,3,1:T(8,128)S(1)}, u32[]{:S(2)}) copy-start(f32[19,4,18,128]{2,0,3,1:T(8,128)S(1)} %pad_maximum_fusion) | copy-start | bytes 2101252
  54.9 14.6 %collective-permute-start.2 = (f32[19,4,18,1]{2,0,3,1:T(8,128)S(1)}, f32[19,4,18,1]{2,0,3,1:T(8,128)S(1)}, u32[]{:S(2)}, u32[]{:S(2)}) collective-permute-start(f32[19,4,18,1]{2,0,3,1:T(8,128)S(1)} %get-tuple-element.22), channel_id=1, source_target_pairs={{1,0},{2,1},{3,2},{4,3},{5,4},{6,5},{7,6},{9,8},{10,9},{11,10},{12... | collective-permute-start | bytes 16424 | tf_op jit(solution)/shard_map/ppermute | solution.py:69
  56.2 14.0 %collective-permute-start.3 = (f32[19,4,18,1]{2,0,3,1:T(8,128)S(1)}, f32[19,4,18,1]{2,0,3,1:T(8,128)}, u32[]{:S(2)}, u32[]{:S(2)}) collective-permute-start(f32[19,4,18,1]{2,0,3,1:T(8,128)S(1)} %get-tuple-element.21), channel_id=1, source_target_pairs={{0,1},{1,2},{2,3},{3,4},{4,5},{5,6},{6,7},{8,9},{9,10},{10,11},{11... | collective-permute-start | bytes 16424 | tf_op jit(solution)/shard_map/ppermute | solution.py:67
  78.6 13.1 %copy-start.6 = (f32[8192]{0:T(1024)S(1)}, f32[8192]{0:T(1024)}, u32[]{:S(2)}) copy-start(f32[8192]{0:T(1024)} %get-tuple-element.129) | copy-start | bytes 98308
  78.7 13.1 %copy-start.12 = (f32[19,19]{1,0:T(8,128)S(1)}, f32[19,19]{1,0:T(8,128)}, u32[]{:S(2)}) copy-start(f32[19,19]{1,0:T(8,128)} %constant.16.clone) | copy-start | bytes 4336
  78.7 13.1 %copy-start.16 = (f32[19]{0:T(128)S(1)}, f32[19]{0:T(128)}, u32[]{:S(2)}) copy-start(f32[19]{0:T(128)} %constant.53.clone) | copy-start | bytes 232
  86.1 8.2 %collective-permute-start.4 = (f32[19,4,1,128]{3,2,1,0:T(1,128)S(1)}, f32[19,4,1,128]{3,2,1,0:T(1,128)S(1)}, u32[]{:S(2)}, u32[]{:S(2)}) collective-permute-start(f32[19,4,1,128]{3,2,1,0:T(1,128)S(1)} %get-tuple-element.86), channel_id=1, source_target_pairs={{8,0},{16,8},{24,16},{9,1},{17,9},{25,17},{10,2},{18,10},{26,18},{... | collective-permute-start | bytes 116744 | tf_op jit(solution)/shard_map/ppermute | solution.py:69
  87.4 11.1 %collective-permute-start.5 = (f32[19,4,1,128]{3,2,1,0:T(1,128)S(1)}, f32[19,4,1,128]{3,2,1,0:T(1,128)S(1)}, u32[]{:S(2)}, u32[]{:S(2)}) collective-permute-start(f32[19,4,1,128]{3,2,1,0:T(1,128)S(1)} %get-tuple-element.85), channel_id=1, source_target_pairs={{0,8},{8,16},{16,24},{1,9},{9,17},{17,25},{2,10},{10,18},{18,26},{... | collective-permute-start | bytes 116744 | tf_op jit(solution)/shard_map/ppermute | solution.py:67
  99.5 7.9 %collective-permute-start.6 = (f32[19,4,18,1]{0,1,3,2:T(4,128)S(1)}, f32[19,4,18,1]{0,1,3,2:T(4,128)S(1)}, u32[]{:S(2)}, u32[]{:S(2)}) collective-permute-start(f32[19,4,18,1]{0,1,3,2:T(4,128)S(1)} %copy.96), channel_id=1, source_target_pairs={{1,0},{2,1},{3,2},{4,3},{5,4},{6,5},{7,6},{9,8},{10,9},{11,10},{12... | collective-permute-start | bytes 16424 | tf_op jit(solution)/shard_map/ppermute | solution.py:69
  101.4 7.1 %collective-permute-start.7 = (f32[19,4,18,1]{0,1,3,2:T(4,128)S(1)}, f32[19,4,18,1]{0,1,3,2:T(4,128)}, u32[]{:S(2)}, u32[]{:S(2)}) collective-permute-start(f32[19,4,18,1]{0,1,3,2:T(4,128)S(1)} %copy.98), channel_id=1, source_target_pairs={{0,1},{1,2},{2,3},{3,4},{4,5},{5,6},{6,7},{8,9},{9,10},{10,11},{11... | collective-permute-start | bytes 16424 | tf_op jit(solution)/shard_map/ppermute | solution.py:67
  106.6 6.2 %copy-start.9 = (f32[1,8192]{1,0:T(1,128)S(1)}, f32[1,8192]{1,0:T(1,128)}, u32[]{:S(2)}) copy-start(f32[1,8192]{1,0:T(1,128)} %slice.694) | copy-start | bytes 98308
  106.6 8.6 %copy-start.3 = (f32[8192]{0:T(1024)S(1)}, f32[8192]{0:T(1024)}, u32[]{:S(2)}) copy-start(f32[8192]{0:T(1024)} %get-tuple-element.130) | copy-start | bytes 98308
  106.6 8.6 %copy-start.5 = (f32[8192]{0:T(1024)S(1)}, f32[8192]{0:T(1024)}, u32[]{:S(2)}) copy-start(f32[8192]{0:T(1024)} %broadcast_multiply_fusion) | copy-start | bytes 98308
  110.5 9.5 %copy-start.8 = (s32[4,16,128]{2,1,0:T(8,128)S(1)}, s32[4,16,128]{2,1,0:T(8,128)}, u32[]{:S(2)}) copy-start(s32[4,16,128]{2,1,0:T(8,128)} %param.15) | copy-start | bytes 98308
  112.6 5.1 %copy-start.2 = (f32[19,8192]{1,0:T(8,128)S(1)}, f32[19,8192]{1,0:T(8,128)}, u32[]{:S(2)}) copy-start(f32[19,8192]{1,0:T(8,128)} %gather_fusion.1) | copy-start | bytes 1867780
  117.7 71.7 %copy-start.14 = (s32[16,128]{1,0:T(8,128)S(1)}, s32[16,128]{1,0:T(8,128)}, u32[]{:S(2)}) copy-start(s32[16,128]{1,0:T(8,128)} %param.16) | copy-start | bytes 24580
  120.0 5.2 %collective-permute-start.8 = (f32[1,128]{1,0:T(1,128)S(1)}, f32[1,128]{1,0:T(1,128)S(1)}, u32[]{:S(2)}, u32[]{:S(2)}) collective-permute-start(f32[1,128]{1,0:T(1,128)S(1)} %get-tuple-element.109), channel_id=1, source_target_pairs={{0,8},{8,16},{16,24},{1,9},{9,17},{17,25},{2,10},{10,18},{18,26},{... | collective-permute-start | bytes 1544 | tf_op jit(solution)/shard_map/ppermute | solution.py:67
  123.9 3.3 %collective-permute-start.9 = (f32[1,128]{1,0:T(1,128)S(1)}, f32[1,128]{1,0:T(1,128)S(1)}, u32[]{:S(2)}, u32[]{:S(2)}) collective-permute-start(f32[1,128]{1,0:T(1,128)S(1)} %get-tuple-element.110), channel_id=1, source_target_pairs={{8,0},{16,8},{24,16},{9,1},{17,9},{25,17},{10,2},{18,10},{26,18},{... | collective-permute-start | bytes 1544 | tf_op jit(solution)/shard_map/ppermute | solution.py:69
  127.3 5.8 %collective-permute-start.10 = (f32[18,1]{1,0:T(8,128)S(1)}, f32[18,1]{1,0:T(8,128)S(1)}, u32[]{:S(2)}, u32[]{:S(2)}) collective-permute-start(f32[18,1]{1,0:T(8,128)S(1)} %get-tuple-element.101), channel_id=1, source_target_pairs={{0,1},{1,2},{2,3},{3,4},{4,5},{5,6},{6,7},{8,9},{9,10},{10,11},{11... | collective-permute-start | bytes 224 | tf_op jit(solution)/shard_map/ppermute | solution.py:67
  131.7 6.3 %collective-permute-start.11 = (f32[18,1]{1,0:T(8,128)S(1)}, f32[18,1]{1,0:T(8,128)S(1)}, u32[]{:S(2)}, u32[]{:S(2)}) collective-permute-start(f32[18,1]{1,0:T(8,128)S(1)} %get-tuple-element.102), channel_id=1, source_target_pairs={{1,0},{2,1},{3,2},{4,3},{5,4},{6,5},{7,6},{9,8},{10,9},{11,10},{12... | collective-permute-start | bytes 224 | tf_op jit(solution)/shard_map/ppermute | solution.py:69
  138.1 6.5 %collective-permute-start.12 = (f32[1,128]{1,0:T(1,128)S(1)}, f32[1,128]{1,0:T(1,128)S(1)}, u32[]{:S(2)}, u32[]{:S(2)}) collective-permute-start(f32[1,128]{1,0:T(1,128)S(1)} %get-tuple-element.107), channel_id=1, source_target_pairs={{0,8},{8,16},{16,24},{1,9},{9,17},{17,25},{2,10},{10,18},{18,26},{... | collective-permute-start | bytes 1544 | tf_op jit(solution)/shard_map/ppermute | solution.py:67
  141.2 3.7 %collective-permute-start.13 = (f32[1,128]{1,0:T(1,128)S(1)}, f32[1,128]{1,0:T(1,128)S(1)}, u32[]{:S(2)}, u32[]{:S(2)}) collective-permute-start(f32[1,128]{1,0:T(1,128)S(1)} %get-tuple-element.108), channel_id=1, source_target_pairs={{8,0},{16,8},{24,16},{9,1},{17,9},{25,17},{10,2},{18,10},{26,18},{... | collective-permute-start | bytes 1544 | tf_op jit(solution)/shard_map/ppermute | solution.py:69
  145.1 6.2 %collective-permute-start.14 = (f32[18,1]{1,0:T(8,128)S(1)}, f32[18,1]{1,0:T(8,128)S(1)}, u32[]{:S(2)}, u32[]{:S(2)}) collective-permute-start(f32[18,1]{1,0:T(8,128)S(1)} %get-tuple-element.99), channel_id=1, source_target_pairs={{0,1},{1,2},{2,3},{3,4},{4,5},{5,6},{6,7},{8,9},{9,10},{10,11},{11... | collective-permute-start | bytes 224 | tf_op jit(solution)/shard_map/ppermute | solution.py:67
  149.9 5.6 %collective-permute-start.15 = (f32[18,1]{1,0:T(8,128)S(1)}, f32[18,1]{1,0:T(8,128)S(1)}, u32[]{:S(2)}, u32[]{:S(2)}) collective-permute-start(f32[18,1]{1,0:T(8,128)S(1)} %get-tuple-element.100), channel_id=1, source_target_pairs={{1,0},{2,1},{3,2},{4,3},{5,4},{6,5},{7,6},{9,8},{10,9},{11,10},{12... | collective-permute-start | bytes 224 | tf_op jit(solution)/shard_map/ppermute | solution.py:69
  155.6 4.1 %collective-permute-start.16 = (f32[1,128]{1,0:T(1,128)S(1)}, f32[1,128]{1,0:T(1,128)S(1)}, u32[]{:S(2)}, u32[]{:S(2)}) collective-permute-start(f32[1,128]{1,0:T(1,128)S(1)} %get-tuple-element.105), channel_id=1, source_target_pairs={{0,8},{8,16},{16,24},{1,9},{9,17},{17,25},{2,10},{10,18},{18,26},{... | collective-permute-start | bytes 1544 | tf_op jit(solution)/shard_map/ppermute | solution.py:67
  158.4 4.9 %collective-permute-start.17 = (f32[1,128]{1,0:T(1,128)S(1)}, f32[1,128]{1,0:T(1,128)S(1)}, u32[]{:S(2)}, u32[]{:S(2)}) collective-permute-start(f32[1,128]{1,0:T(1,128)S(1)} %get-tuple-element.106), channel_id=1, source_target_pairs={{8,0},{16,8},{24,16},{9,1},{17,9},{25,17},{10,2},{18,10},{26,18},{... | collective-permute-start | bytes 1544 | tf_op jit(solution)/shard_map/ppermute | solution.py:69
  163.3 4.3 %collective-permute-start.18 = (f32[18,1]{1,0:T(8,128)S(1)}, f32[18,1]{1,0:T(8,128)S(1)}, u32[]{:S(2)}, u32[]{:S(2)}) collective-permute-start(f32[18,1]{1,0:T(8,128)S(1)} %get-tuple-element.97), channel_id=1, source_target_pairs={{0,1},{1,2},{2,3},{3,4},{4,5},{5,6},{6,7},{8,9},{9,10},{10,11},{11... | collective-permute-start | bytes 224 | tf_op jit(solution)/shard_map/ppermute | solution.py:67
  166.3 5.6 %collective-permute-start.19 = (f32[18,1]{1,0:T(8,128)S(1)}, f32[18,1]{1,0:T(8,128)S(1)}, u32[]{:S(2)}, u32[]{:S(2)}) collective-permute-start(f32[18,1]{1,0:T(8,128)S(1)} %get-tuple-element.98), channel_id=1, source_target_pairs={{1,0},{2,1},{3,2},{4,3},{5,4},{6,5},{7,6},{9,8},{10,9},{11,10},{12... | collective-permute-start | bytes 224 | tf_op jit(solution)/shard_map/ppermute | solution.py:69
  171.9 7.2 %collective-permute-start.20 = (f32[1,128]{1,0:T(1,128)S(1)}, f32[1,128]{1,0:T(1,128)S(1)}, u32[]{:S(2)}, u32[]{:S(2)}) collective-permute-start(f32[1,128]{1,0:T(1,128)S(1)} %get-tuple-element.103), channel_id=1, source_target_pairs={{0,8},{8,16},{16,24},{1,9},{9,17},{17,25},{2,10},{10,18},{18,26},{... | collective-permute-start | bytes 1544 | tf_op jit(solution)/shard_map/ppermute | solution.py:67
  175.1 4.1 %collective-permute-start.21 = (f32[1,128]{1,0:T(1,128)S(1)}, f32[1,128]{1,0:T(1,128)S(1)}, u32[]{:S(2)}, u32[]{:S(2)}) collective-permute-start(f32[1,128]{1,0:T(1,128)S(1)} %get-tuple-element.104), channel_id=1, source_target_pairs={{8,0},{16,8},{24,16},{9,1},{17,9},{25,17},{10,2},{18,10},{26,18},{... | collective-permute-start | bytes 1544 | tf_op jit(solution)/shard_map/ppermute | solution.py:69
  179.2 5.9 %collective-permute-start.22 = (f32[18,1]{1,0:T(8,128)S(1)}, f32[18,1]{1,0:T(8,128)S(1)}, u32[]{:S(2)}, u32[]{:S(2)}) collective-permute-start(f32[18,1]{1,0:T(8,128)S(1)} %get-tuple-element.95), channel_id=1, source_target_pairs={{0,1},{1,2},{2,3},{3,4},{4,5},{5,6},{6,7},{8,9},{9,10},{10,11},{11... | collective-permute-start | bytes 224 | tf_op jit(solution)/shard_map/ppermute | solution.py:67
  183.8 5.6 %collective-permute-start.23 = (f32[18,1]{1,0:T(8,128)S(1)}, f32[18,1]{1,0:T(8,128)S(1)}, u32[]{:S(2)}, u32[]{:S(2)}) collective-permute-start(f32[18,1]{1,0:T(8,128)S(1)} %get-tuple-element.96), channel_id=1, source_target_pairs={{1,0},{2,1},{3,2},{4,3},{5,4},{6,5},{7,6},{9,8},{10,9},{11,10},{12... | collective-permute-start | bytes 224 | tf_op jit(solution)/shard_map/ppermute | solution.py:69
where the time goes:
time: 241 us; the launch traced here: 238 us
  starting transfers between devices  62.9 us (26%)
  local copies, waits for them, and re-layouts  58.2 us (24%)
  blocking collectives  42 us (17%)
  other arithmetic  28.2 us (12%)
  waiting for transfers between devices  23.8 us (10%)
  matrix products  21.7 us (9%)
    ppermute x12, starting transfers between devices, extended(): lax.ppermute(tail, axis, [(i, (i + 1) % count) for i in range(ends)])  47.5 us
    psum x1, blocking collectives, per_device(): lax.psum((jnp.stack([jnp.sum(smooth * region_one), jnp.sum(smooth * regio...  42 us
    ppermute x12, waiting for transfers between devices, extended(): lax.ppermute(head, axis, [((i + 1) % count, i) for i in range(ends)])  23.5 us
    ppermute x12, starting transfers between devices, extended(): lax.ppermute(head, axis, [((i + 1) % count, i) for i in range(ends)])  15.5 us
    unnamed x45, local copies, waits for them, and re-layouts  12.3 us
    concatenate x3, local copies, waits for them, and re-layouts, extended(): jnp.concatenate([lax.ppermute(tail, axis, [(i, (i + 1) % count) for i in...  9.7 us
    dot_general x4, matrix products, collide(): jnp.dot(relax_matrix, popul - equilib, precision=lax.Precision.HIGHEST)  9.56 us
    ppermute x4, local copies, waits for them, and re-layouts, extended(): lax.ppermute(tail, axis, [(i, (i + 1) % count) for i in range(ends)])  9.16 us
  transfers between devices with their start and end apart: 24, of which 11 were waited for; matrix products, arithmetic and copies ran while one was open for 19% of the time, Pallas kernels for 0%

commit v1 on v0

v1 whole, which is shorter than its diff:
```python
import functools

import jax
import jax.numpy as jnp
from jax import lax
from jax.experimental import pallas as pl
from jax.experimental.pallas import tpu as pltpu
from jax.sharding import PartitionSpec as P

SWEEPS = 4
VELOCITIES = [
    (0, 0, 0),
    (1, 0, 0),
    (-1, 0, 0),
    (0, 1, 0),
    (0, -1, 0),
    (0, 0, 1),
    (0, 0, -1),
    (1, 1, 0),
    (-1, -1, 0),
    (1, -1, 0),
    (-1, 1, 0),
    (1, 0, 1),
    (-1, 0, -1),
    (1, 0, -1),
    (-1, 0, 1),
    (0, 1, 1),
    (0, -1, -1),
    (0, 1, -1),
    (0, -1, 1),
]
PAIRS = [VELOCITIES[2 * k + 1] for k in range(9)]
BLOCK_LIMIT = 0.5
SENSE_SCALE = 20.0
FILTER_WEIGHT = 16.0
MESH = pl.DeviceIdType.MESH
F32 = jnp.float32

DIRS = [(-1, 0), (1, 0), (0, -1), (0, 1), (-1, -1), (-1, 1), (1, -1), (1, 1)]


def pops_with(cx=None, cy=None):
    return [
        i
        for i, v in enumerate(VELOCITIES)
        if (cx is None or v[0] == cx) and (cy is None or v[1] == cy)
    ]


def add_all(terms):
    terms = list(terms)
    while len(terms) > 1:
        terms = [
            terms[k] + terms[k + 1] if k + 1 < len(terms) else terms[k]
            for k in range(0, len(terms), 2)
        ]
    return terms[0]


def along(values, axis):
    total = None
    for vel, val in zip(PAIRS, values):
        if vel[axis] == 0:
            continue
        if total is None:
            total = val if vel[axis] > 0 else -val
        else:
            total = total + val if vel[axis] > 0 else total - val
    return total


def dotted(vec, vel):
    total = None
    for comp, c in zip(vec, vel):
        if c == 0:
            continue
        if total is None:
            total = comp if c > 0 else -comp
        else:
            total = total + comp if c > 0 else total - comp
    return total


def adjoint_cell(f, a, blocking):
    fe = [f[2 * k + 1] + f[2 * k + 2] for k in range(9)]
    fo = [f[2 * k + 1] - f[2 * k + 2] for k in range(9)]
    rho = add_all([f[0]] + fe)
    inv = 1.0 / rho
    u = [along(fo, d) * inv for d in range(3)]
    usq = u[0] * u[0] + u[1] * u[1] + u[2] * u[2]

    e = [a[2 * k + 1] + a[2 * k + 2] for k in range(9)]
    o = [a[2 * k + 1] - a[2 * k + 2] for k in range(9)]
    mom = [0.28 * along(o, d) for d in range(3)]
    big_o = [1.4 * o[k] - dotted(mom, PAIRS[k]) for k in range(9)]
    edge = [e[3] + e[4], e[5] + e[6], e[7] + e[8]]
    axis_sum = e[0] + e[1] + e[2]
    edge_sum = edge[0] + edge[1] + edge[2]
    mean16 = (1.6 / 19.0) * (a[0] + axis_sum + edge_sum)
    a4 = 4.0 * a[0]
    t = [
        edge[0] - 2.0 * (e[0] + e[1]) + a4,
        edge[1] - 2.0 * (e[0] + e[2]) + a4,
        edge[2] - 2.0 * (e[1] + e[2]) + a4,
    ]
    tsum = (2.0 / 7.0) * (t[0] + t[1] + t[2])
    p = [(0.4 / 12.0) * (tk - tsum) for tk in t]
    b0 = 1.6 * a[0] - mean16 - 4.0 * (p[0] + p[1] + p[2])
    q = [-2.0 * (p[0] + p[1]), -2.0 * (p[0] + p[2]), -2.0 * (p[1] + p[2])]
    shift = [2.0 * (mean16 + val) for val in q + p]
    plane = [0, 1, 2, 3, 3, 4, 4, 5, 5]
    big_e = [1.6 * e[k] - shift[plane[k]] for k in range(9)]

    c36 = 1.0 / 36.0
    s3, s5, s7 = big_e[3] + big_e[4], big_e[5] + big_e[6], big_e[7] + big_e[8]
    zeroth = (1.0 / 3.0) * b0 + c36 * (
        2.0 * (big_e[0] + big_e[1] + big_e[2]) + s3 + s5 + s7
    )
    xx = c36 * (2.0 * big_e[0] + s3 + s5)
    yy = c36 * (2.0 * big_e[1] + s3 + s7)
    zz = c36 * (2.0 * big_e[2] + s5 + s7)
    xy = c36 * (big_e[3] - big_e[4])
    xz = c36 * (big_e[5] - big_e[6])
    yz = c36 * (big_e[7] - big_e[8])
    weighted = [2.0 * big_o[k] if k < 3 else big_o[k] for k in range(9)]
    first = [c36 * along(weighted, d) for d in range(3)]
    bu = [
        xx * u[0] + xy * u[1] + xz * u[2],
        xy * u[0] + yy * u[1] + yz * u[2],
        xz * u[0] + yz * u[1] + zz * u[2],
    ]
    ubu = 4.5 * (u[0] * bu[0] + u[1] * bu[1] + u[2] * bu[2])
    half_u = 1.5 * usq * zeroth
    scalar = zeroth + half_u - ubu
    vec = [3.0 * (first[d] - zeroth * u[d]) + 9.0 * bu[d] for d in range(3)]
    eq_b = zeroth - half_u + ubu + 3.0 * (
        first[0] * u[0] + first[1] * u[1] + first[2] * u[2]
    )

    open_part = 1.0 - blocking
    odd_keep = 1.0 - 2.0 * blocking
    result = [None] * 19
    result[0] = a[0] + open_part * (scalar - b0)
    half_open = 0.5 * open_part
    half_keep = 0.5 * odd_keep
    scalar2 = 2.0 * scalar
    vec2 = [2.0 * val for val in vec]
    for k in range(9):
        even = 0.5 * e[k] + half_open * (scalar2 - big_e[k])
        odd = half_keep * o[k] + half_open * (dotted(vec2, PAIRS[k]) - big_o[k])
        result[2 * k + 1] = even + odd
        result[2 * k + 2] = even - odd
    parts = [b0 * f[0] - rho * eq_b]
    for k in range(9):
        parts.append(0.5 * (big_e[k] * fe[k] + big_o[k] * fo[k]) - fo[k] * o[k])
    return result, add_all(parts)


def kernel(
    nx,
    ny,
    adj_hbm,
    pops_hbm,
    solid_hbm,
    label_hbm,
    design_hbm,
    out_ref,
    sens_ref,
    adj,
    pops,
    solid,
    label,
    design,
    mid,
    pull,
    send1,
    recv1,
    send2,
    recv2,
    send3,
    recv3,
    gath1,
    gath2,
    part1,
    part2,
    in_sem,
    s_sem,
    r_sem,
    g1s_sem,
    g1r_sem,
    g2s_sem,
    g2r_sem,
):
    mx, my = lax.axis_index("gx"), lax.axis_index("gy")

    def has(d):
        conds = []
        if d[0] < 0:
            conds.append(mx > 0)
        if d[0] > 0:
            conds.append(mx < nx - 1)
        if d[1] < 0:
            conds.append(my > 0)
        if d[1] > 0:
            conds.append(my < ny - 1)
        return functools.reduce(jnp.logical_and, conds)

    barrier = pltpu.get_barrier_semaphore()
    for k in range(1, nx):
        pl.semaphore_signal(
            barrier, inc=1, device_id=(lax.rem(mx + k, nx), my), device_id_type=MESH
        )
    for k in range(1, ny):
        pl.semaphore_signal(
            barrier, inc=1, device_id=(mx, lax.rem(my + k, ny)), device_id_type=MESH
        )
    for d in DIRS[4:]:

        @pl.when(has(d))
        def _():
            pl.semaphore_signal(
                barrier, inc=1, device_id=(mx + d[0], my + d[1]), device_id_type=MESH
            )

    loads = [
        pltpu.make_async_copy(src, dst, in_sem.at[k])
        for k, (src, dst) in enumerate(
            [
                (adj_hbm, adj),
                (label_hbm, label),
                (pops_hbm, pops),
                (solid_hbm, solid),
                (design_hbm, design),
            ]
        )
    ]
    for load in loads:
        load.start()

    for n, d in enumerate(DIRS):

        @pl.when(jnp.logical_not(has((-d[0], -d[1]))))
        def _():
            for buf in (recv1, recv2, recv3):
                buf[n] = jnp.zeros(buf.shape[1:], F32)

    lane = lax.broadcasted_iota(jnp.int32, (16, 128), 1)
    lane4 = lax.broadcasted_iota(jnp.int32, (4, 128), 1)

    def copies(rnd, send, recv):
        out = []
        for n, d in enumerate(DIRS):
            rows = {0: (32, 16, 16), 1: (24, 16, 8), 2: (8, 16, 8)}[rnd][
                0 if d[1] == 0 else (1 if d[0] == 0 else 2)
            ]
            start = 0
            if rnd == 2 and d[0] > 0:
                start = 8
            src = send.at[pl.ds(start, rows)] if rnd == 2 else send.at[n, pl.ds(0, rows)]
            out.append(
                pltpu.make_async_remote_copy(
                    src_ref=src,
                    dst_ref=recv.at[n, pl.ds(0, rows)],
                    send_sem=s_sem.at[rnd, n],
                    recv_sem=r_sem.at[rnd, n],
                    device_id=(mx + d[0], my + d[1]),
                    device_id_type=MESH,
                )
            )
        return out

    def start_all(cps):
        for n, d in enumerate(DIRS):

            @pl.when(has(d))
            def _():
                cps[n].start()

    def recv_all(cps):
        for n, d in enumerate(DIRS):

            @pl.when(has((-d[0], -d[1])))
            def _():
                cps[n].wait_recv()

    def send_done(cps):
        for n, d in enumerate(DIRS):

            @pl.when(has(d))
            def _():
                cps[n].wait_send()

    def pack(src, send, region):
        for n, (dx, dy) in enumerate(DIRS):
            if dy == 0:
                row = 0 if dx < 0 else 15
                for j, i in enumerate(pops_with(cx=-dx)):
                    for z in range(4):
                        send[n, 4 * j + z : 4 * j + z + 1] = src[i, z, row : row + 1, :]
                if region is not None:
                    send[n, 24:32] = region[0:8] if dx < 0 else region[8:16]
            elif dx == 0:
                at = 0 if dy < 0 else 127
                base = 64 if dy < 0 else 0
                acc = region if region is not None else jnp.zeros((16, 128), F32)
                for j, i in enumerate(pops_with(cy=-dy)):
                    for z in range(4):
                        to = base + 4 * j + z
                        moved = pltpu.roll(src[i, z], (to - at) % 128, 1)
                        acc = jnp.where(lane == to, moved, acc)
                send[n, 0:16] = acc
            else:
                row = 0 if dx < 0 else 15
                i = VELOCITIES.index((-dx, -dy, 0))
                for z in range(4):
                    send[n, z : z + 1] = src[i, z, row : row + 1, :]
                if region is not None:
                    send[n, 8:16] = region[0:8] if dx < 0 else region[8:16]

    def pull_local(src):
        for i, (cx, cy, cz) in enumerate(VELOCITIES):
            for z in range(4):
                val = src[i, z]
                if cy != 0:
                    val = pltpu.roll(val, (-cy) % 128, 1)
                pull[i, z, 8:24] = val

    def pull_edges(recv):
        for n, (dx, dy) in enumerate(DIRS):
            if dx == 0:
                base = 64 if dy < 0 else 0
                at = 127 if dy < 0 else 0
                got = recv[n, 0:16]
                for j, i in enumerate(pops_with(cy=-dy)):
                    for z in range(4):
                        moved = pltpu.roll(got, (at - base - 4 * j - z) % 128, 1)
                        pull[i, z, 8:24] = jnp.where(lane == at, moved, pull[i, z, 8:24])
            elif dy == 0:
                row = 24 if dx < 0 else 7
                for j, i in enumerate(pops_with(cx=-dx)):
                    cy = VELOCITIES[i][1]
                    val = recv[n, 4 * j : 4 * j + 4]
                    if cy != 0:
                        val = pltpu.roll(val, (-cy) % 128, 1)
                        corner = recv[DIRS.index((dx, -cy)), 0:4]
                        corner = pltpu.roll(corner, (-cy) % 128, 1)
                        val = jnp.where(lane4 == (127 if cy > 0 else 0), corner, val)
                    for z in range(4):
                        pull[i, z, row : row + 1] = val[z : z + 1]

    def cells(section, dst):
        total = None
        for z in range(4):
            f = [pops[section, i, z].astype(F32) for i in range(19)]
            a = []
            for i, (cx, cy, cz) in enumerate(VELOCITIES):
                a.append(pull[i, (z + cz) % 4, 8 + cx : 24 + cx, :])
            is_solid = solid[z] == 1
            inside = label[...] > 0
            blocking = jnp.where(
                is_solid, 1.0, jnp.where(inside, BLOCK_LIMIT * design[...], 0.0)
            )
            lever = jnp.where(
                jnp.logical_and(jnp.logical_not(is_solid), inside), BLOCK_LIMIT, 0.0
            )
            result, term = adjoint_cell(f, a, blocking)
            for i in range(19):
                dst[i, z] = result[i]
            term = term * lever
            total = term if total is None else total + term
        return total

    wide_row = lax.broadcasted_iota(jnp.int32, (32, 256), 0)
    wide_lane = lax.broadcasted_iota(jnp.int32, (32, 256), 1)
    gone = jnp.logical_or(
        jnp.logical_or(
            jnp.logical_and(wide_row >= 24, mx == 0),
            jnp.logical_and(
                jnp.logical_and(wide_row >= 16, wide_row < 24), mx == nx - 1
            ),
        ),
        jnp.logical_or(
            jnp.logical_and(wide_lane >= 192, my == 0),
            jnp.logical_and(
                jnp.logical_and(wide_lane >= 128, wide_lane < 192), my == ny - 1
            ),
        ),
    )
    scale_den = 1.0 / (1.0 + 4.0 * FILTER_WEIGHT)
    keep = jnp.where(gone, 0.0, scale_den)

    def widened(own, get):
        low = lane[0:8] < 64
        top = jnp.concatenate(
            [own, jnp.where(lane < 64, get((0, -1)), get((0, 1)))], axis=1
        )
        down = jnp.concatenate(
            [get((-1, 0)), jnp.where(low, get((-1, -1)), get((-1, 1)))], axis=1
        )
        up = jnp.concatenate(
            [get((1, 0)), jnp.where(low, get((1, -1)), get((1, 1)))], axis=1
        )
        return jnp.concatenate([top, down, up], axis=0)

    def jacobi(start):
        base = start * keep
        weight = FILTER_WEIGHT * keep
        smooth = jnp.where(gone, 0.0, start)
        for _ in range(SWEEPS):
            beside = (
                pltpu.roll(smooth, 1, 0)
                + pltpu.roll(smooth, 31, 0)
                + pltpu.roll(smooth, 1, 1)
                + pltpu.roll(smooth, 255, 1)
            )
            smooth = base + weight * beside
        return smooth

    loads[0].wait()
    loads[1].wait()
    region = label[...].astype(F32)
    pack(adj, send1, region)
    met = (nx - 1) + (ny - 1)
    for d in DIRS[4:]:
        met = met + has(d).astype(jnp.int32)
    pl.semaphore_wait(barrier, met)
    cps1 = copies(0, send1, recv1)
    start_all(cps1)
    pull_local(adj)
    for load in loads[2:]:
        load.wait()
    recv_all(cps1)
    pull_edges(recv1)
    raw1 = cells(1, mid)

    pack(mid, send2, None)
    cps2 = copies(1, send2, recv2)
    start_all(cps2)
    pull_local(mid)

    def label_of(d):
        n = DIRS.index(d)
        if d[1] == 0:
            return recv1[n, 24:32]
        if d[0] == 0:
            return recv1[n, 0:16]
        return recv1[n, 8:16]

    wide_label = widened(region, label_of)
    share = []
    for r in (1.0, 2.0):
        share.append(jacobi(jnp.where(wide_label == r, 1.0, 0.0))[0:16, 0:128])

    def folded(one, two):
        one = jnp.sum(one, axis=0, keepdims=True)
        two = jnp.sum(two, axis=0, keepdims=True)
        one = one + pltpu.roll(one, 64, 1)
        two = two + pltpu.roll(two, 64, 1)
        return jnp.where(lane[0:1] < 64, one, two)

    part1[...] = jnp.zeros((8, 128), F32)
    part1[1:2] = folded(jnp.where(region == 1.0, 1.0, 0.0), jnp.where(region == 2.0, 1.0, 0.0))

    recv_all(cps2)
    pull_edges(recv2)
    raw2 = cells(0, out_ref)
    raw = SENSE_SCALE * (raw1 + raw2)
    send3[...] = raw
    part1[0:1] = folded(raw * share[0], raw * share[1])

    def gather(part, slots, send_sem, recv_sem, count, along_x):
        out = []
        for k in range(1, count):
            if along_x:
                peer = (lax.rem(mx + k, count), my)
            else:
                peer = (mx, lax.rem(my + k, count))
            out.append(
                pltpu.make_async_remote_copy(
                    src_ref=part,
                    dst_ref=slots.at[k - 1],
                    send_sem=send_sem.at[k - 1],
                    recv_sem=recv_sem.at[k - 1],
                    device_id=peer,
                    device_id_type=MESH,
                )
            )
        return out

    g1 = gather(part1, gath1, g1s_sem, g1r_sem, nx, True)
    for cp in g1:
        cp.start()
    cps3 = copies(2, send3, recv3)
    start_all(cps3)
    total = part1[...]
    for k, cp in enumerate(g1):
        cp.wait_recv()
        total = total + gath1[k]
    part2[...] = total
    g2 = gather(part2, gath2, g2s_sem, g2r_sem, ny, False)
    for cp in g2:
        cp.start()

    recv_all(cps3)

    def raw_of(d):
        n = DIRS.index(d)
        return recv3[n, 0:16] if d[0] == 0 else recv3[n, 0:8]

    smooth = jacobi(widened(raw, raw_of))[0:16, 0:128]
    for k, cp in enumerate(g2):
        cp.wait_recv()
        total = total + gath2[k]
    lane8 = lane[0:8] < 64
    ones = jnp.sum(jnp.where(lane8, total, 0.0), axis=1, keepdims=True)
    twos = jnp.sum(jnp.where(lane8, 0.0, total), axis=1, keepdims=True)
    mean1 = ones[0:1] / jnp.maximum(ones[1:2], 1.0)
    mean2 = twos[0:1] / jnp.maximum(twos[1:2], 1.0)
    sens_ref[...] = jnp.where(
        region == 1.0, smooth - mean1, jnp.where(region == 2.0, smooth - mean2, 0.0)
    )
    send_done(cps1)
    send_done(cps2)
    send_done(cps3)
    for cp in g1 + g2:
        cp.wait_send()


def per_device(nx, ny, adjoint_in, forward_pops, solid_mask, region_label, design):
    vmem, dma = pltpu.VMEM, pltpu.SemaphoreType.DMA
    return pl.pallas_call(
        functools.partial(kernel, nx, ny),
        out_shape=(
            jax.ShapeDtypeStruct(adjoint_in.shape, F32),
            jax.ShapeDtypeStruct(design.shape, F32),
        ),
        in_specs=[pl.BlockSpec(memory_space=pl.ANY)] * 5,
        out_specs=(
            pl.BlockSpec(memory_space=pltpu.VMEM),
            pl.BlockSpec(memory_space=pltpu.VMEM),
        ),
        scratch_shapes=[
            vmem(adjoint_in.shape, F32),
            vmem(forward_pops.shape, jnp.bfloat16),
            vmem(solid_mask.shape, jnp.int32),
            vmem(region_label.shape, jnp.int32),
            vmem(design.shape, F32),
            vmem(adjoint_in.shape, F32),
            vmem((19, 4, 32, 128), F32),
            vmem((8, 32, 128), F32),
            vmem((8, 32, 128), F32),
            vmem((8, 24, 128), F32),
            vmem((8, 24, 128), F32),
            vmem((16, 128), F32),
            vmem((8, 16, 128), F32),
            vmem((nx - 1, 8, 128), F32),
            vmem((ny - 1, 8, 128), F32),
            vmem((8, 128), F32),
            vmem((8, 128), F32),
            dma((5,)),
            dma((3, 8)),
            dma((3, 8)),
            dma((nx - 1,)),
            dma((nx - 1,)),
            dma((ny - 1,)),
            dma((ny - 1,)),
        ],
        compiler_params=pltpu.CompilerParams(
            collective_id=0, has_side_effects=True, vmem_limit_bytes=40 * 1024 * 1024
        ),
    )(adjoint_in, forward_pops, solid_mask, region_label, design)


def solution(mesh):
    in_specs = (
        P(None, None, "gx", "gy"),
        P(None, None, None, "gx", "gy"),
        P(None, "gx", "gy"),
        P("gx", "gy"),
        P("gx", "gy"),
    )
    out_specs = (P(None, None, "gx", "gy"), P("gx", "gy"))
    return jax.shard_map(
        functools.partial(per_device, mesh.shape["gx"], mesh.shape["gy"]),
        mesh=mesh,
        in_specs=in_specs,
        out_specs=out_specs,
        check_vma=False,
    )
```

time: 241 us -> 27.2 us (0.11)
  starting transfers between devices: 62.9 us -> 0 us
  local copies, waits for them, and re-layouts: 58.2 us -> 5.72 us
  blocking collectives: 42 us -> 0 us
  other arithmetic: 28.2 us -> 0 us
  waiting for transfers between devices: 23.8 us -> 0 us
  matrix products: 21.7 us -> 0 us
  Pallas kernels: 0 us -> 20.4 us
    ppermute x24 -> x0, starting transfers between devices: 62.9 us -> none  [the longest x12 47.5 us: extended(): lax.ppermute(tail, axis, [(i, (i + 1) % count) for i in range(ends)])]
    psum x1 -> x0, blocking collectives: 42 us -> none  [per_device(): lax.psum((jnp.stack([jnp.sum(smooth * region_one), jnp.sum(smooth * regio...]
    ppermute x24 -> x0, waiting for transfers between devices: 23.8 us -> none  [the longest x12 23.5 us: extended(): lax.ppermute(head, axis, [((i + 1) % count, i) for i in range(ends)])]
    dot_general x12 -> x0, matrix products: 21.7 us -> none  [the longest x4 9.56 us: collide(): jnp.dot(relax_matrix, popul - equilib, precision=lax.Precision.HIGHEST)]
    pallas_call x0 -> x1, Pallas kernels: none -> 20.4 us  [per_device(): pl.pallas_call(functools.partial(kernel, nx, ny), out_shape=(jax.ShapeDty...]
    ppermute x8 -> x0, local copies, waits for them, and re-layouts: 16.6 us -> none  [the longest x4 9.16 us: extended(): lax.ppermute(tail, axis, [(i, (i + 1) % count) for i in range(ends)])]
    concatenate x24 -> x0, other arithmetic: 11.6 us -> none  [the longest x7 8.5 us: extended(): jnp.concatenate([lax.ppermute(tail, axis, [(i, (i + 1) % count) for i in...]
    slice x25 -> x0, local copies, waits for them, and re-layouts: 10.8 us -> none  [the longest x6 3.1 us: pull_back(): pieces.append(jnp.roll(piece, -step_z, axis=0))]
  transfers between devices with their start and end apart: 24 -> 0, of which waited for: 11 -> 0; matrix products, arithmetic and copies ran while one was open for 19% -> 0% of each run, Pallas kernels for 0% -> 0%
where the time goes in v1:
time: 27.2 us; the launch traced here: 26.8 us
  Pallas kernels  20.4 us (75%)
  local copies, waits for them, and re-layouts  5.72 us (21%)
  between operations  0.65 us (2%)
    pallas_call x1, Pallas kernels, per_device(): pl.pallas_call(functools.partial(kernel, nx, ny), out_shape=(jax.ShapeDty...  20.4 us
    unnamed x12, local copies, waits for them, and re-layouts  5.72 us

profile of v1, /device:TPU:0, one launch (start us, length us, event | category | flops | bytes accessed | tf_op | source)
XLA Modules:
  0.0 26.8 jit_solution(4571182069951230215)
XLA Ops:
  0.6 0.0 copy-start
  0.6 1.1 %copy-done = f32[19,4,16,128]{3,2,1,0:T(8,128)S(1)} copy-done((f32[19,4,16,128]{3,2,1,0:T(8,128)S(1)}, f32[19,4,16,128]{3,2,1,0:T(8,128)}, u32[]{:S(2)}) %copy-start) | copy-done | bytes 622616
  1.7 0.0 copy-start.1
  1.7 1.1 %copy-done.1 = bf16[2,19,4,16,128]{4,3,2,1,0:T(8,128)(2,1)S(1)} copy-done((bf16[2,19,4,16,128]{4,3,2,1,0:T(8,128)(2,1)S(1)}, bf16[2,19,4,16,128]{4,3,2,1,0:T(8,128)(2,1)}, u32[]{:S(2)}) %copy-start.1) | copy-done | bytes 622616
  2.8 0.0 copy-start.2
  2.8 0.8 %copy-done.2 = s32[4,16,128]{2,1,0:T(8,128)S(1)} copy-done((s32[4,16,128]{2,1,0:T(8,128)S(1)}, s32[4,16,128]{2,1,0:T(8,128)}, u32[]{:S(2)}) %copy-start.2) | copy-done | bytes 32792
  3.5 0.0 copy-start.3
  3.5 0.7 %copy-done.3 = s32[16,128]{1,0:T(8,128)S(1)} copy-done((s32[16,128]{1,0:T(8,128)S(1)}, s32[16,128]{1,0:T(8,128)}, u32[]{:S(2)}) %copy-start.3) | copy-done | bytes 8216
  4.2 0.0 copy-start.4
  4.2 0.7 %copy-done.4 = f32[16,128]{1,0:T(8,128)S(1)} copy-done((f32[16,128]{1,0:T(8,128)S(1)}, f32[16,128]{1,0:T(8,128)}, u32[]{:S(2)}) %copy-start.4) | copy-done | bytes 8216
  4.9 20.4 %shard_map.68 = (f32[19,4,16,128]{3,2,1,0:T(8,128)S(1)}, f32[16,128]{1,0:T(8,128)S(1)}) custom-call(f32[19,4,16,128]{3,2,1,0:T(8,128)S(1)} %copy-done, bf16[2,19,4,16,128]{4,3,2,1,0:T(8,128)(2,1)S(1)} %copy-done.1, s32[4,16,128]{2,1,0:T(8,128)S(1)} %copy-done.2, s32[16,128]{1,0:T(8,128)S(1)} %copy-done.3, f32[16,128]{1,0:T(8,128)S(1)} %copy-done.4), custom_call_target="tpu_custom_call" | custom-call | tf_op jit(solution)/shard_map/pallas_call | solution.py:531
  25.4 0.8 %copy.9 = f32[19,4,16,128]{3,2,1,0:T(8,128)} copy(f32[19,4,16,128]{3,2,1,0:T(8,128)S(1)} %get-tuple-element.4) | data formatting | bytes 1245184
  26.2 0.6 %copy.10 = f32[16,128]{1,0:T(8,128)} copy(f32[16,128]{1,0:T(8,128)S(1)} %get-tuple-element.5) | data formatting | bytes 16384
Async XLA Ops:
  0.6 1.1 %copy-start = (f32[19,4,16,128]{3,2,1,0:T(8,128)S(1)}, f32[19,4,16,128]{3,2,1,0:T(8,128)}, u32[]{:S(2)}) copy-start(f32[19,4,16,128]{3,2,1,0:T(8,128)} %adj_hbm.1) | copy-start | bytes 1867780
  1.7 1.1 %copy-start.1 = (bf16[2,19,4,16,128]{4,3,2,1,0:T(8,128)(2,1)S(1)}, bf16[2,19,4,16,128]{4,3,2,1,0:T(8,128)(2,1)}, u32[]{:S(2)}) copy-start(bf16[2,19,4,16,128]{4,3,2,1,0:T(8,128)(2,1)} %pops_hbm.1) | copy-start | bytes 1867780
  2.8 0.8 %copy-start.2 = (s32[4,16,128]{2,1,0:T(8,128)S(1)}, s32[4,16,128]{2,1,0:T(8,128)}, u32[]{:S(2)}) copy-start(s32[4,16,128]{2,1,0:T(8,128)} %solid_hbm.1) | copy-start | bytes 98308
  3.5 0.7 %copy-start.3 = (s32[16,128]{1,0:T(8,128)S(1)}, s32[16,128]{1,0:T(8,128)}, u32[]{:S(2)}) copy-start(s32[16,128]{1,0:T(8,128)} %label_hbm.1) | copy-start | bytes 24580
  4.2 0.7 %copy-start.4 = (f32[16,128]{1,0:T(8,128)S(1)}, f32[16,128]{1,0:T(8,128)}, u32[]{:S(2)}) copy-start(f32[16,128]{1,0:T(8,128)} %design_hbm.1) | copy-start | bytes 24580

commit v2 on v1

--- a/solution.py
+++ b/solution.py
@@ -179,17 +179,13 @@
     recv2,
     send3,
     recv3,
-    gath1,
-    gath2,
-    part1,
-    part2,
+    gath,
+    part,
     in_sem,
     s_sem,
     r_sem,
-    g1s_sem,
-    g1r_sem,
-    g2s_sem,
-    g2r_sem,
+    gs_sem,
+    gr_sem,
 ):
     mx, my = lax.axis_index("gx"), lax.axis_index("gy")
 
@@ -206,21 +202,26 @@
         return functools.reduce(jnp.logical_and, conds)
 
     barrier = pltpu.get_barrier_semaphore()
-    for k in range(1, nx):
-        pl.semaphore_signal(
-            barrier, inc=1, device_id=(lax.rem(mx + k, nx), my), device_id_type=MESH
-        )
-    for k in range(1, ny):
-        pl.semaphore_signal(
-            barrier, inc=1, device_id=(mx, lax.rem(my + k, ny)), device_id_type=MESH
-        )
-    for d in DIRS[4:]:
-
-        @pl.when(has(d))
-        def _():
-            pl.semaphore_signal(
-                barrier, inc=1, device_id=(mx + d[0], my + d[1]), device_id_type=MESH
-            )
+    count = nx * ny
+    mine = mx * ny + my
+
+    def peer(k):
+        flat = lax.rem(mine + k, count)
+        return (flat // ny, lax.rem(flat, ny))
+
+    def each_peer(body):
+        if count <= 64:
+            for k in range(1, count):
+                body(k)
+        else:
+
+            @pl.loop(1, count)
+            def _(k):
+                body(k)
+
+    @each_peer
+    def _(k):
+        pl.semaphore_signal(barrier, inc=1, device_id=peer(k), device_id_type=MESH)
 
     loads = [
         pltpu.make_async_copy(src, dst, in_sem.at[k])
@@ -420,10 +421,7 @@
     loads[1].wait()
     region = label[...].astype(F32)
     pack(adj, send1, region)
-    met = (nx - 1) + (ny - 1)
-    for d in DIRS[4:]:
-        met = met + has(d).astype(jnp.int32)
-    pl.semaphore_wait(barrier, met)
+    pl.semaphore_wait(barrier, count - 1)
     cps1 = copies(0, send1, recv1)
     start_all(cps1)
     pull_local(adj)
@@ -451,55 +449,46 @@
     for r in (1.0, 2.0):
         share.append(jacobi(jnp.where(wide_label == r, 1.0, 0.0))[0:16, 0:128])
 
-    def folded(one, two):
-        one = jnp.sum(one, axis=0, keepdims=True)
-        two = jnp.sum(two, axis=0, keepdims=True)
-        one = one + pltpu.roll(one, 64, 1)
-        two = two + pltpu.roll(two, 64, 1)
-        return jnp.where(lane[0:1] < 64, one, two)
-
-    part1[...] = jnp.zeros((8, 128), F32)
-    part1[1:2] = folded(jnp.where(region == 1.0, 1.0, 0.0), jnp.where(region == 2.0, 1.0, 0.0))
+    quarter = lax.broadcasted_iota(jnp.int32, (1, 128), 1) // 32
+
+    def folded(vals):
+        row = jnp.zeros((1, 128), F32)
+        for k, val in enumerate(vals):
+            val = jnp.sum(val, axis=0, keepdims=True)
+            val = val + pltpu.roll(val, 64, 1)
+            val = val + pltpu.roll(val, 32, 1)
+            row = jnp.where(quarter == k, val, row)
+        return row
+
+    zero = jnp.zeros((16, 128), F32)
+    counts = folded(
+        [zero, zero, jnp.where(region == 1.0, 1.0, 0.0), jnp.where(region == 2.0, 1.0, 0.0)]
+    )
 
     recv_all(cps2)
     pull_edges(recv2)
     raw2 = cells(0, out_ref)
     raw = SENSE_SCALE * (raw1 + raw2)
     send3[...] = raw
-    part1[0:1] = folded(raw * share[0], raw * share[1])
-
-    def gather(part, slots, send_sem, recv_sem, count, along_x):
-        out = []
-        for k in range(1, count):
-            if along_x:
-                peer = (lax.rem(mx + k, count), my)
-            else:
-                peer = (mx, lax.rem(my + k, count))
-            out.append(
-                pltpu.make_async_remote_copy(
-                    src_ref=part,
-                    dst_ref=slots.at[k - 1],
-                    send_sem=send_sem.at[k - 1],
-                    recv_sem=recv_sem.at[k - 1],
-                    device_id=peer,
-                    device_id_type=MESH,
-                )
-            )
-        return out
-
-    g1 = gather(part1, gath1, g1s_sem, g1r_sem, nx, True)
-    for cp in g1:
-        cp.start()
+
     cps3 = copies(2, send3, recv3)
     start_all(cps3)
-    total = part1[...]
-    for k, cp in enumerate(g1):
-        cp.wait_recv()
-        total = total + gath1[k]
-    part2[...] = total
-    g2 = gather(part2, gath2, g2s_sem, g2r_sem, ny, False)
-    for cp in g2:
-        cp.start()
+    own_sums = folded([raw * share[0], raw * share[1]]) + counts
+    part[...] = own_sums
+
+    def sums_to(k):
+        return pltpu.make_async_remote_copy(
+            src_ref=part,
+            dst_ref=gath.at[k - 1],
+            send_sem=gs_sem.at[k - 1],
+            recv_sem=gr_sem.at[k - 1],
+            device_id=peer(k),
+            device_id_type=MESH,
+        )
+
+    @each_peer
+    def _(k):
+        sums_to(k).start()
 
     recv_all(cps3)
 
@@ -508,22 +497,27 @@
         return recv3[n, 0:16] if d[0] == 0 else recv3[n, 0:8]
 
     smooth = jacobi(widened(raw, raw_of))[0:16, 0:128]
-    for k, cp in enumerate(g2):
-        cp.wait_recv()
-        total = total + gath2[k]
-    lane8 = lane[0:8] < 64
-    ones = jnp.sum(jnp.where(lane8, total, 0.0), axis=1, keepdims=True)
-    twos = jnp.sum(jnp.where(lane8, 0.0, total), axis=1, keepdims=True)
-    mean1 = ones[0:1] / jnp.maximum(ones[1:2], 1.0)
-    mean2 = twos[0:1] / jnp.maximum(twos[1:2], 1.0)
+
+    @each_peer
+    def _(k):
+        sums_to(k).wait_recv()
+
+    total = own_sums + jnp.sum(gath[...], axis=0)
+    tot = [
+        jnp.sum(jnp.where(quarter == k, total, 0.0), axis=1, keepdims=True) for k in range(4)
+    ]
+    mean1 = tot[0] / jnp.maximum(tot[2], 1.0)
+    mean2 = tot[1] / jnp.maximum(tot[3], 1.0)
     sens_ref[...] = jnp.where(
         region == 1.0, smooth - mean1, jnp.where(region == 2.0, smooth - mean2, 0.0)
     )
     send_done(cps1)
     send_done(cps2)
     send_done(cps3)
-    for cp in g1 + g2:
-        cp.wait_send()
+
+    @each_peer
+    def _(k):
+        sums_to(k).wait_send()
 
 
 def per_device(nx, ny, adjoint_in, forward_pops, solid_mask, region_label, design):
@@ -534,7 +528,7 @@
             jax.ShapeDtypeStruct(adjoint_in.shape, F32),
             jax.ShapeDtypeStruct(design.shape, F32),
         ),
-        in_specs=[pl.BlockSpec(memory_space=pl.ANY)] * 5,
+        in_specs=[pl.BlockSpec(memory_space=pltpu.HBM)] * 5,
         out_specs=(
             pl.BlockSpec(memory_space=pltpu.VMEM),
             pl.BlockSpec(memory_space=pltpu.VMEM),
@@ -553,22 +547,23 @@
             vmem((8, 24, 128), F32),
             vmem((16, 128), F32),
             vmem((8, 16, 128), F32),
-            vmem((nx - 1, 8, 128), F32),
-            vmem((ny - 1, 8, 128), F32),
-            vmem((8, 128), F32),
-            vmem((8, 128), F32),
+            vmem((nx * ny - 1, 1, 128), F32),
+            vmem((1, 128), F32),
             dma((5,)),
             dma((3, 8)),
             dma((3, 8)),
-            dma((nx - 1,)),
-            dma((nx - 1,)),
-            dma((ny - 1,)),
-            dma((ny - 1,)),
+            dma((nx * ny - 1,)),
+            dma((nx * ny - 1,)),
         ],
         compiler_params=pltpu.CompilerParams(
             collective_id=0, has_side_effects=True, vmem_limit_bytes=40 * 1024 * 1024
         ),
-    )(adjoint_in, forward_pops, solid_mask, region_label, design)
+    )(
+        *(
+            pltpu.with_memory_space_constraint(arg, pltpu.HBM)
+            for arg in (adjoint_in, forward_pops, solid_mask, region_label, design)
+        )
+    )
 
 
 def solution(mesh):

time: 27.2 us -> 21.8 us (0.80)
  local copies, waits for them, and re-layouts: 5.72 us -> 1.43 us
  Pallas kernels: 20.4 us -> 19.6 us
    unnamed x12 -> x2, local copies, waits for them, and re-layouts: 5.72 us -> 1.43 us
    pallas_call x1, Pallas kernels: 20.4 us -> 19.6 us  [per_device(): pl.pallas_call(functools.partial(kernel, nx, ny), out_shape=(jax.ShapeDty...]
where the time goes in v2:
time: 21.8 us; the launch traced here: 21.7 us
  Pallas kernels  19.6 us (90%)
  local copies, waits for them, and re-layouts  1.43 us (7%)
  between operations  0.64 us (3%)
    pallas_call x1, Pallas kernels, per_device(): pl.pallas_call(functools.partial(kernel, nx, ny), out_shape=(jax.ShapeDty...  19.6 us
    unnamed x2, local copies, waits for them, and re-layouts  1.43 us

profile of v2, /device:TPU:0, one launch (start us, length us, event | category | flops | bytes accessed | tf_op | source)
XLA Modules:
  0.0 21.7 jit_solution(3474846590050549643)
XLA Ops:
  0.6 19.6 %shard_map.68 = (f32[19,4,16,128]{3,2,1,0:T(8,128)S(1)}, f32[16,128]{1,0:T(8,128)S(1)}) custom-call(f32[19,4,16,128]{3,2,1,0:T(8,128)} %adj_hbm.1, bf16[2,19,4,16,128]{4,3,2,1,0:T(8,128)(2,1)} %pops_hbm.1, s32[4,16,128]{2,1,0:T(8,128)} %solid_hbm.1, s32[16,128]{1,0:T(8,128)} %label_hbm.1, f32[16,128]{1,0:T(8,128)} %design_hbm.1), custom_call_target="tpu_custom_call" | custom-call | tf_op jit(solution)/shard_map/pallas_call | solution.py:525
  20.2 0.8 %copy.9 = f32[19,4,16,128]{3,2,1,0:T(8,128)} copy(f32[19,4,16,128]{3,2,1,0:T(8,128)S(1)} %get-tuple-element.4) | data formatting | bytes 1245184
  21.1 0.6 %copy.10 = f32[16,128]{1,0:T(8,128)} copy(f32[16,128]{1,0:T(8,128)S(1)} %get-tuple-element.5) | data formatting | bytes 16384

commit v3 on v2

--- a/solution.py
+++ b/solution.py
@@ -205,30 +205,14 @@
     count = nx * ny
     mine = mx * ny + my
 
-    def peer(k):
-        flat = lax.rem(mine + k, count)
-        return (flat // ny, lax.rem(flat, ny))
-
-    def each_peer(body):
-        if count <= 64:
-            for k in range(1, count):
-                body(k)
-        else:
-
-            @pl.loop(1, count)
-            def _(k):
-                body(k)
-
-    @each_peer
-    def _(k):
-        pl.semaphore_signal(barrier, inc=1, device_id=peer(k), device_id_type=MESH)
-
     loads = [
         pltpu.make_async_copy(src, dst, in_sem.at[k])
         for k, (src, dst) in enumerate(
             [
-                (adj_hbm, adj),
                 (label_hbm, label),
+                (adj_hbm.at[pl.ds(0, 7)], adj.at[pl.ds(0, 7)]),
+                (adj_hbm.at[pl.ds(7, 6)], adj.at[pl.ds(7, 6)]),
+                (adj_hbm.at[pl.ds(13, 6)], adj.at[pl.ds(13, 6)]),
                 (pops_hbm, pops),
                 (solid_hbm, solid),
                 (design_hbm, design),
@@ -237,6 +221,27 @@
     ]
     for load in loads:
         load.start()
+
+    def wrapped(pos, step, size):
+        to = pos + step
+        return jnp.where(to >= size, to - size, to)
+
+    peer_x = [wrapped(mx, k, nx) for k in range(nx)]
+    peer_y = [wrapped(my, k, ny) for k in range(ny)]
+
+    def each_peer(body):
+        if count <= 64:
+            for k in range(1, count):
+                body(k, (peer_x[k // ny], peer_y[k % ny]))
+        else:
+
+            @pl.loop(1, count)
+            def _(k):
+                body(k, (wrapped(mx, k // ny, nx), wrapped(my, lax.rem(k, ny), ny)))
+
+    @each_peer
+    def _(k, peer):
+        pl.semaphore_signal(barrier, inc=1, device_id=peer, device_id_type=MESH)
 
     for n, d in enumerate(DIRS):
 
@@ -417,15 +422,15 @@
             smooth = base + weight * beside
         return smooth
 
-    loads[0].wait()
-    loads[1].wait()
+    for load in loads[:4]:
+        load.wait()
     region = label[...].astype(F32)
     pack(adj, send1, region)
     pl.semaphore_wait(barrier, count - 1)
     cps1 = copies(0, send1, recv1)
     start_all(cps1)
     pull_local(adj)
-    for load in loads[2:]:
+    for load in loads[4:]:
         load.wait()
     recv_all(cps1)
     pull_edges(recv1)
@@ -476,20 +481,19 @@
     own_sums = folded([raw * share[0], raw * share[1]]) + counts
     part[...] = own_sums
 
-    def sums_to(k):
-        return pltpu.make_async_remote_copy(
+    @each_peer
+    def _(k, peer):
+        pltpu.make_async_remote_copy(
             src_ref=part,
             dst_ref=gath.at[k - 1],
-            send_sem=gs_sem.at[k - 1],
-            recv_sem=gr_sem.at[k - 1],
-            device_id=peer(k),
+            send_sem=gs_sem.at[0],
+            recv_sem=gr_sem.at[0],
+            device_id=peer,
             device_id_type=MESH,
-        )
-
-    @each_peer
-    def _(k):
-        sums_to(k).start()
-
+        ).start()
+
+    send_done(cps1)
+    send_done(cps2)
     recv_all(cps3)
 
     def raw_of(d):
@@ -498,10 +502,9 @@
 
     smooth = jacobi(widened(raw, raw_of))[0:16, 0:128]
 
-    @each_peer
-    def _(k):
-        sums_to(k).wait_recv()
-
+    send_done(cps3)
+    pltpu.make_async_copy(gath, gath, gs_sem.at[0]).wait()
+    pltpu.make_async_copy(gath, gath, gr_sem.at[0]).wait()
     total = own_sums + jnp.sum(gath[...], axis=0)
     tot = [
         jnp.sum(jnp.where(quarter == k, total, 0.0), axis=1, keepdims=True) for k in range(4)
@@ -511,13 +514,6 @@
     sens_ref[...] = jnp.where(
         region == 1.0, smooth - mean1, jnp.where(region == 2.0, smooth - mean2, 0.0)
     )
-    send_done(cps1)
-    send_done(cps2)
-    send_done(cps3)
-
-    @each_peer
-    def _(k):
-        sums_to(k).wait_send()
 
 
 def per_device(nx, ny, adjoint_in, forward_pops, solid_mask, region_label, design):
@@ -549,11 +545,11 @@
             vmem((8, 16, 128), F32),
             vmem((nx * ny - 1, 1, 128), F32),
             vmem((1, 128), F32),
-            dma((5,)),
+            dma((7,)),
             dma((3, 8)),
             dma((3, 8)),
-            dma((nx * ny - 1,)),
-            dma((nx * ny - 1,)),
+            dma((1,)),
+            dma((1,)),
         ],
         compiler_params=pltpu.CompilerParams(
             collective_id=0, has_side_effects=True, vmem_limit_bytes=40 * 1024 * 1024

time: 21.8 us -> 21.1 us (0.968)
  Pallas kernels: 19.6 us -> 18.8 us
    pallas_call x1, Pallas kernels: 19.6 us -> 18.8 us  [per_device(): pl.pallas_call(functools.partial(kernel, nx, ny), out_shape=(jax.ShapeDty...]
where the time goes in v3:
time: 21.1 us; the launch traced here: 20.9 us
  Pallas kernels  18.8 us (89%)
  local copies, waits for them, and re-layouts  1.43 us (7%)
  between operations  0.64 us (3%)
    pallas_call x1, Pallas kernels, per_device(): pl.pallas_call(functools.partial(kernel, nx, ny), out_shape=(jax.ShapeDty...  18.8 us
    unnamed x2, local copies, waits for them, and re-layouts  1.43 us

profile of v3, /device:TPU:0, one launch (start us, length us, event | category | flops | bytes accessed | tf_op | source)
XLA Modules:
  0.0 20.9 jit_solution(9462329168588130750)
XLA Ops:
  0.6 18.8 %shard_map.68 = (f32[19,4,16,128]{3,2,1,0:T(8,128)S(1)}, f32[16,128]{1,0:T(8,128)S(1)}) custom-call(f32[19,4,16,128]{3,2,1,0:T(8,128)} %adj_hbm.1, bf16[2,19,4,16,128]{4,3,2,1,0:T(8,128)(2,1)} %pops_hbm.1, s32[4,16,128]{2,1,0:T(8,128)} %solid_hbm.1, s32[16,128]{1,0:T(8,128)} %label_hbm.1, f32[16,128]{1,0:T(8,128)} %design_hbm.1), custom_call_target="tpu_custom_call" | custom-call | tf_op jit(solution)/shard_map/pallas_call | solution.py:521
  19.5 0.8 %copy.9 = f32[19,4,16,128]{3,2,1,0:T(8,128)} copy(f32[19,4,16,128]{3,2,1,0:T(8,128)S(1)} %get-tuple-element.4) | data formatting | bytes 1245184
  20.3 0.6 %copy.10 = f32[16,128]{1,0:T(8,128)} copy(f32[16,128]{1,0:T(8,128)S(1)} %get-tuple-element.5) | data formatting | bytes 16384

commit v4 on v3

--- a/solution.py
+++ b/solution.py
@@ -296,8 +296,9 @@
             def _():
                 cps[n].wait_send()
 
-    def pack(src, send, region):
-        for n, (dx, dy) in enumerate(DIRS):
+    def pack(src, send, region, cps=None):
+        for n in (2, 3, 0, 1, 4, 5, 6, 7):
+            dx, dy = DIRS[n]
             if dy == 0:
                 row = 0 if dx < 0 else 15
                 for j, i in enumerate(pops_with(cx=-dx)):
@@ -322,6 +323,11 @@
                     send[n, z : z + 1] = src[i, z, row : row + 1, :]
                 if region is not None:
                     send[n, 8:16] = region[0:8] if dx < 0 else region[8:16]
+            if cps is not None:
+
+                @pl.when(has((dx, dy)))
+                def _():
+                    cps[n].start()
 
     def pull_local(src):
         for i, (cx, cy, cz) in enumerate(VELOCITIES):
@@ -436,9 +442,8 @@
     pull_edges(recv1)
     raw1 = cells(1, mid)
 
-    pack(mid, send2, None)
     cps2 = copies(1, send2, recv2)
-    start_all(cps2)
+    pack(mid, send2, None, cps2)
     pull_local(mid)
 
     def label_of(d):
@@ -476,8 +481,6 @@
     raw = SENSE_SCALE * (raw1 + raw2)
     send3[...] = raw
 
-    cps3 = copies(2, send3, recv3)
-    start_all(cps3)
     own_sums = folded([raw * share[0], raw * share[1]]) + counts
     part[...] = own_sums
 
@@ -492,6 +495,8 @@
             device_id_type=MESH,
         ).start()
 
+    cps3 = copies(2, send3, recv3)
+    start_all(cps3)
     send_done(cps1)
     send_done(cps2)
     recv_all(cps3)

time: 21.1 us -> 21 us (level)
  no operation moved by 1% of the time
where the time goes in v4:
time: 21 us; the launch traced here: 20.8 us
  Pallas kernels  18.8 us (90%)
  local copies, waits for them, and re-layouts  1.43 us (7%)
  between operations  0.64 us (3%)
    pallas_call x1, Pallas kernels, per_device(): pl.pallas_call(functools.partial(kernel, nx, ny), out_shape=(jax.ShapeDty...  18.8 us
    unnamed x2, local copies, waits for them, and re-layouts  1.43 us

profile of v4, /device:TPU:0, one launch (start us, length us, event | category | flops | bytes accessed | tf_op | source)
XLA Modules:
  0.0 20.8 jit_solution(8474195150977544968)
XLA Ops:
  0.6 18.8 %shard_map.68 = (f32[19,4,16,128]{3,2,1,0:T(8,128)S(1)}, f32[16,128]{1,0:T(8,128)S(1)}) custom-call(f32[19,4,16,128]{3,2,1,0:T(8,128)} %adj_hbm.1, bf16[2,19,4,16,128]{4,3,2,1,0:T(8,128)(2,1)} %pops_hbm.1, s32[4,16,128]{2,1,0:T(8,128)} %solid_hbm.1, s32[16,128]{1,0:T(8,128)} %label_hbm.1, f32[16,128]{1,0:T(8,128)} %design_hbm.1), custom_call_target="tpu_custom_call" | custom-call | tf_op jit(solution)/shard_map/pallas_call | solution.py:526
  19.4 0.8 %copy.9 = f32[19,4,16,128]{3,2,1,0:T(8,128)} copy(f32[19,4,16,128]{3,2,1,0:T(8,128)S(1)} %get-tuple-element.4) | data formatting | bytes 1245184
  20.2 0.6 %copy.10 = f32[16,128]{1,0:T(8,128)} copy(f32[16,128]{1,0:T(8,128)S(1)} %get-tuple-element.5) | data formatting | bytes 16384
